TPU v7x, 32 devices: a whole 2x2x4 slice. The times are simulated.
32 devices in a mesh: cd: 8 (over z, y), ab: 4 (over x, core).
Axes of the slice: x: 2, y: 2, z: 4, core: 2. Of those that a mesh axis runs over, the one named last changes fastest.
Arguments:
- amplitudes: bfloat16 [512, 8, 800], P('cd', None, 'ab'), may hold values from -6 to 6
- integrals: bfloat16 [8, 800, 2048], P('cd', None, 'ab'), may hold values from -0.078125 to 0.078125
Outputs:
- ladder: float32 [512, 2048], P('cd', 'ab')
All inputs are finite; a program needn't handle non-finite values.
Results may differ from a plain program's by a relative error of at most 0.0003.
Values may be sent and summed in bfloat16 or wider, within the bound.
A program may use at most 64 MiB of HBM per device.

v0:
```python
import jax
import jax.numpy as jnp
from jax import lax
from jax.sharding import PartitionSpec as P


def on_device(amplitudes, integrals):
    c_local, d_width, ab_local = integrals.shape
    assembled = lax.all_gather(amplitudes, "ab", axis=2, tiled=True)
    complete = lax.all_to_all(assembled, "cd", split_axis=1, concat_axis=0, tiled=True)
    flat = complete.reshape(complete.shape[0], c_local * d_width)
    slab = integrals.reshape(c_local * d_width, ab_local)
    return lax.psum_scatter(
        jnp.dot(flat, slab, preferred_element_type=jnp.float32),
        "cd",
        scatter_dimension=0,
        tiled=True,
    )


def solution(mesh):
    in_specs = (P("cd", None, "ab"), P("cd", None, "ab"))
    out_specs = P("cd", "ab")
    return jax.shard_map(
        on_device, mesh=mesh, in_specs=in_specs, out_specs=out_specs, check_vma=False
    )
```

profile of v0, /device:TPU:0, one launch (start us, length us, event | category | flops | bytes accessed | tf_op | source)
XLA Modules:
  0.0 125.0 jit_solution(4527043416997278588)
XLA Ops:
  6.5 0.0 copy-start
  6.5 0.0 reduce-scatter.2.cloned.1.call-start
  6.5 1.4 %copy.4 = bf16[64,8,200]{0,1,2:T(8,128)(2,1)S(1)} copy(bf16[64,8,200]{2,1,0:T(8,128)(2,1)} %param.2) | data formatting | bytes 409600 | tf_op args[0]
  8.0 14.7 %all_gather.3 = bf16[64,8,800]{0,1,2:T(8,128)(2,1)S(1)} all-gather(bf16[64,8,200]{0,1,2:T(8,128)(2,1)S(1)} %copy.4), channel_id=1, replica_groups=mesh['cd'=8,'ab'=4] {'ab'}, dimensions={2}, use_global_device_ids=true | all-gather | bytes 1024000 | tf_op jit(solution)/shard_map/all_gather | solution.py:9
  22.6 1.9 %copy.5 = bf16[64,8,800]{2,0,1:T(8,128)(2,1)S(1)} copy(bf16[64,8,800]{0,1,2:T(8,128)(2,1)S(1)} %all_gather.3) | data formatting | bytes 1638400 | tf_op jit(solution)/shard_map/all_gather | solution.py:9
  24.6 29.4 %all_to_all.15 = bf16[64,8,800]{2,0,1:T(8,128)(2,1)S(1)} all-to-all(bf16[64,8,800]{2,0,1:T(8,128)(2,1)S(1)} %copy.5), channel_id=1, replica_groups=mesh['cd'=8,'ab'=4] {'cd'}, dimensions={1} | all-to-all | bytes 1638400 | tf_op jit(solution)/shard_map/all_to_all | solution.py:10
  54.0 0.0 copy-done
  54.0 1.7 %fusion = f32[512,512]{1,0:T(8,128)} fusion(bf16[512,800]{1,0:T(8,128)(2,1)S(1)} %bitcast.9, bf16[1,800,512]{2,1,0:T(8,128)(2,1)S(1)} %copy-done), kind=kOutput, calls=%fused_computation | convolution fusion | flops 419430400 | bytes 2686976 | tf_op jit(solution)/shard_map/dot_general | solution.py:14
  55.7 0.0 reduce-scatter.2.cloned.1.call-update
  55.7 62.4 %reduce-scatter.2.cloned.1.call-done = f32[64,512]{1,0:T(8,128)} async-done(((f32[512,512]{1,0:T(8,128)}), f32[64,512]{1,0:T(8,128)}) %reduce-scatter.2.cloned.1.call-update) | async-done | bytes 131088 | tf_op jit(solution)/shard_map/reduce_scatter | solution.py:13
Async XLA Ops:
  6.5 47.5 %copy-start = (bf16[1,800,512]{2,1,0:T(8,128)(2,1)S(1)}, bf16[1,800,512]{2,1,0:T(8,128)(2,1)}, u32[]{:S(2)}) copy-start(bf16[1,800,512]{2,1,0:T(8,128)(2,1)} %param.3) | copy-start | bytes 2457604
  6.5 111.6 %reduce-scatter.2.cloned.1.call-start = ((), (), s32[]{:S(2)}) async-start(), calls=%async_computation.2 | async-start | bytes 1179648 | tf_op jit(solution)/shard_map/reduce_scatter | solution.py:13
Sparse Core Ops, SparseCore 0:
  55.8 62.2 reduce-scatter.1
where the time goes:
time: 125 us
  waiting for transfers between devices  62.4 us (50%)
  blocking collectives  44.1 us (35%)
  between operations  13.4 us (11%)
  local copies, waits for them, and re-layouts  3.34 us (3%)
  matrix products  1.68 us (1%)
    reduce_scatter x1, waiting for transfers between devices, on_device(): lax.psum_scatter(jnp.dot(flat, slab, preferred_element_type=jnp.float32),...  62.4 us
    all_to_all x1, blocking collectives, on_device(): lax.all_to_all(assembled, 'cd', split_axis=1, concat_axis=0, tiled=True)  29.4 us
    all_gather x1, blocking collectives, on_device(): assembled = lax.all_gather(amplitudes, 'ab', axis=2, tiled=True)  14.7 us
  transfers between devices with their start and end apart: 1, of which 1 were waited for; matrix products, arithmetic and copies ran while one was open for 0% of the time, Pallas kernels for 0%

commit v1 on v0

--- a/solution.py
+++ b/solution.py
@@ -7,7 +7,19 @@
 def on_device(amplitudes, integrals):
     c_local, d_width, ab_local = integrals.shape
     assembled = lax.all_gather(amplitudes, "ab", axis=2, tiled=True)
-    complete = lax.all_to_all(assembled, "cd", split_axis=1, concat_axis=0, tiled=True)
+    ways, here = (lax.axis_size("cd"), lax.axis_index("cd"))
+    width = assembled.shape[1] // ways
+    shape = list(assembled.shape)
+    shape[1] = width
+    height = shape[0]
+    shape[0] = height * ways
+    full = jnp.zeros(shape, assembled.dtype)
+    for mask in range(ways):
+        part = lax.dynamic_slice_in_dim(assembled, (here ^ mask) * width, width, axis=1)
+        if mask:
+            part = lax.ppermute(part, "cd", [(d, d ^ mask) for d in range(ways)])
+        full = lax.dynamic_update_slice_in_dim(full, part, (here ^ mask) * height, axis=0)
+    complete = full
     flat = complete.reshape(complete.shape[0], c_local * d_width)
     slab = integrals.reshape(c_local * d_width, ab_local)
     return lax.psum_scatter(

time: 125 us -> 132 us (1.056)
  blocking collectives: 44.1 us -> 14.7 us
  waiting for transfers between devices: 62.4 us -> 75.7 us
  local copies, waits for them, and re-layouts: 3.34 us -> 15 us
  starting transfers between devices: 0.01 us -> 11.4 us
    all_to_all x1 -> x0, blocking collectives: 29.4 us -> none  [on_device(): lax.all_to_all(assembled, 'cd', split_axis=1, concat_axis=0, tiled=True)]
    ppermute x0 -> x7, starting transfers between devices: none -> 11.4 us  [on_device(): part = lax.ppermute(part, 'cd', [(d, d ^ mask) for d in range(ways)])]
    unnamed x3 -> x17, local copies, waits for them, and re-layouts: 1.41 us -> 10.4 us
    ppermute x0 -> x7, waiting for transfers between devices: none -> 8.28 us  [on_device(): part = lax.ppermute(part, 'cd', [(d, d ^ mask) for d in range(ways)])]
    reduce_scatter x1, waiting for transfers between devices: 62.4 us -> 67.4 us  [on_device(): lax.psum_scatter(jnp.dot(flat, slab, preferred_element_type=jnp.float32),...]
    dynamic_slice x0 -> x1, local copies, waits for them, and re-layouts: none -> 4.34 us  [on_device(): lax.dynamic_slice_in_dim(assembled, (here ^ mask) * width, width, axis=1)]
    all_gather x1 -> x0, local copies, waits for them, and re-layouts: 1.93 us -> none  [on_device(): assembled = lax.all_gather(amplitudes, 'ab', axis=2, tiled=True)]
  transfers between devices with their start and end apart: 1 -> 8, of which waited for: 1 -> 2; matrix products, arithmetic and copies ran while one was open for 0% -> 6% of each run, Pallas kernels for 0% -> 0%
where the time goes in v1:
time: 132 us
  waiting for transfers between devices  75.7 us (57%)
  local copies, waits for them, and re-layouts  15 us (11%)
  blocking collectives  14.7 us (11%)
  between operations  13.6 us (10%)
  starting transfers between devices  11.4 us (9%)
  matrix products  1.68 us (1%)
    reduce_scatter x1, waiting for transfers between devices, on_device(): lax.psum_scatter(jnp.dot(flat, slab, preferred_element_type=jnp.float32),...  67.4 us
    all_gather x1, blocking collectives, on_device(): assembled = lax.all_gather(amplitudes, 'ab', axis=2, tiled=True)  14.7 us
    ppermute x7, starting transfers between devices, on_device(): part = lax.ppermute(part, 'cd', [(d, d ^ mask) for d in range(ways)])  11.4 us
    unnamed x17, local copies, waits for them, and re-layouts  10.4 us
    ppermute x7, waiting for transfers between devices, on_device(): part = lax.ppermute(part, 'cd', [(d, d ^ mask) for d in range(ways)])  8.28 us
    dynamic_slice x1, local copies, waits for them, and re-layouts, on_device(): lax.dynamic_slice_in_dim(assembled, (here ^ mask) * width, width, axis=1)  4.34 us
  transfers between devices with their start and end apart: 8, of which 2 were waited for; matrix products, arithmetic and copies ran while one was open for 6% of the time, Pallas kernels for 0%

profile of v1, /device:TPU:0, one launch (start us, length us, event | category | flops | bytes accessed | tf_op | source)
XLA Modules:
  0.0 132.1 jit_solution(8542994861519288075)
XLA Ops:
  6.5 0.0 copy-start
  6.5 0.0 reduce-scatter.2.cloned.1.call-start
  6.5 1.4 %copy.4 = bf16[64,8,200]{0,1,2:T(8,128)(2,1)S(1)} copy(bf16[64,8,200]{2,1,0:T(8,128)(2,1)} %param.2) | data formatting | bytes 409600 | tf_op args[0]
  8.0 14.7 %all_gather.3 = bf16[64,8,800]{0,1,2:T(8,128)(2,1)S(1)} all-gather(bf16[64,8,200]{0,1,2:T(8,128)(2,1)S(1)} %copy.4), channel_id=1, replica_groups=mesh['cd'=8,'ab'=4] {'ab'}, dimensions={2}, use_global_device_ids=true | all-gather | bytes 1024000 | tf_op jit(solution)/shard_map/all_gather | solution.py:9
  22.6 4.3 %constant_dynamic-slice_fusion = (bf16[64,1,800]{0,1,2:T(2,128)(2,1)S(1)}, bf16[64,1,800]{0,1,2:T(2,128)(2,1)S(1)}, bf16[64,1,800]{0,1,2:T(2,128)(2,1)}, bf16[64...) fusion(bf16[64,8,800]{0,1,2:T(8,128)(2,1)S(1)} %all_gather.3, ...), kind=kLoop, calls=%fused_computation.10 | loop fusion | bytes 1638432 | tf_op jit(solution)/shard_map/dynamic_slice | solution.py:18
  27.0 0.0 copy-start.3
  27.0 0.0 copy-start.2
  27.0 0.0 copy-start.1
  27.0 1.9 %copy.14 = bf16[64,1,800]{2,0,1:T(8,128)(2,1)} copy(bf16[64,1,800]{0,1,2:T(2,128)(2,1)} %get-tuple-element.11) | data formatting | bytes 204800
  28.9 1.5 %collective-permute-start = (bf16[64,1,800]{2,0,1:T(8,128)(2,1)}, bf16[64,1,800]{2,0,1:T(8,128)(2,1)S(1)}, u32[]{:S(2)}, u32[]{:S(2)}) collective-permute-start(bf16[64,1,800]{2,0,1:T(8,128)(2,1)} %copy.14), channel_id=1, source_target_pairs={{0,4},{4,0},{8,12},{12,8},{16,20},{20,16},{24,28},{28,24},{1,5},{5... | collective-permute-start | bytes 307208 | tf_op jit(solution)/shard_map/ppermute | solution.py:20
  30.4 1.8 %copy.15 = bf16[64,1,800]{2,0,1:T(8,128)(2,1)} copy(bf16[64,1,800]{0,1,2:T(2,128)(2,1)} %get-tuple-element.10) | data formatting | bytes 204800
  32.2 1.6 %collective-permute-start.1 = (bf16[64,1,800]{2,0,1:T(8,128)(2,1)}, bf16[64,1,800]{2,0,1:T(8,128)(2,1)S(1)}, u32[]{:S(2)}, u32[]{:S(2)}) collective-permute-start(bf16[64,1,800]{2,0,1:T(8,128)(2,1)} %copy.15), channel_id=1, source_target_pairs={{0,8},{4,12},{8,0},{12,4},{16,24},{20,28},{24,16},{28,20},{1,9},{5... | collective-permute-start | bytes 307208 | tf_op jit(solution)/shard_map/ppermute | solution.py:20
  33.8 1.8 %copy.16 = bf16[64,1,800]{2,0,1:T(8,128)(2,1)} copy(bf16[64,1,800]{0,1,2:T(2,128)(2,1)} %get-tuple-element.9) | data formatting | bytes 204800
  35.6 0.4 collective-permute-start.2
  36.0 0.0 copy-done.3
  36.0 0.6 copy.17
  36.6 2.7 %collective-permute-start.3 = (bf16[64,1,800]{2,0,1:T(8,128)(2,1)S(1)}, bf16[64,1,800]{2,0,1:T(8,128)(2,1)S(1)}, u32[]{:S(2)}, u32[]{:S(2)}) collective-permute-start(bf16[64,1,800]{2,0,1:T(8,128)(2,1)S(1)} %copy.17), channel_id=1, source_target_pairs={{0,16},{4,20},{8,24},{12,28},{16,0},{20,4},{24,8},{28,12},{1,17},{... | collective-permute-start | bytes 307208 | tf_op jit(solution)/shard_map/ppermute | solution.py:20
  39.3 0.0 copy-done.2
  39.3 0.6 copy.18
  39.9 1.4 %collective-permute-start.4 = (bf16[64,1,800]{2,0,1:T(8,128)(2,1)S(1)}, bf16[64,1,800]{2,0,1:T(8,128)(2,1)S(1)}, u32[]{:S(2)}, u32[]{:S(2)}) collective-permute-start(bf16[64,1,800]{2,0,1:T(8,128)(2,1)S(1)} %copy.18), channel_id=1, source_target_pairs={{0,20},{4,16},{8,28},{12,24},{16,4},{20,0},{24,12},{28,8},{1,21},{... | collective-permute-start | bytes 307208 | tf_op jit(solution)/shard_map/ppermute | solution.py:20
  41.2 0.0 copy-done.1
  41.2 0.6 copy.13
  41.8 0.1 reshape.38
  42.0 1.2 copy.19
  43.1 0.6 copy.20
  43.8 0.0 collective-permute-done
  43.8 3.7 %collective-permute-start.5 = (bf16[64,1,800]{2,0,1:T(8,128)(2,1)}, bf16[64,1,800]{2,0,1:T(8,128)(2,1)S(1)}, u32[]{:S(2)}, u32[]{:S(2)}) collective-permute-start(bf16[64,1,800]{2,0,1:T(8,128)(2,1)} %copy.19), channel_id=1, source_target_pairs={{0,24},{4,28},{8,16},{12,20},{16,8},{20,12},{24,0},{28,4},{1,25},{... | collective-permute-start | bytes 307208 | tf_op jit(solution)/shard_map/ppermute | solution.py:20
  47.5 0.0 collective-permute-done.1
  47.5 0.2 collective-permute-start.6
  47.7 0.0 collective-permute-done.2
  47.8 0.0 collective-permute-done.3
  47.8 8.3 %collective-permute-done.4 = bf16[64,1,800]{2,0,1:T(8,128)(2,1)S(1)} collective-permute-done((bf16[64,1,800]{2,0,1:T(8,128)(2,1)S(1)}, bf16[64,1,800]{2,0,1:T(8,128)(2,1)S(1)}, u32[]{:S(2)}, u32[]{:S(2)}) %collective-permute-start.4) | collective-permute-done | bytes 102432 | tf_op jit(solution)/shard_map/ppermute | solution.py:20
  56.1 0.0 collective-permute-done.5
  56.1 0.0 collective-permute-done.6
  56.1 0.0 copy-done
  56.2 1.7 %fusion = f32[512,512]{1,0:T(8,128)} fusion(bf16[512,800]{1,0:T(8,128)(2,1)S(1)} %bitcast_dynamic-update-slice_fusion, bf16[1,800,512]{2,1,0:T(8,128)(2,1)S(1)} %copy-done), kind=kOutput, calls=%fused_computation | convolution fusion | flops 419430400 | bytes 2686976 | tf_op jit(solution)/shard_map/dot_general | solution.py:26
  57.8 0.0 reduce-scatter.2.cloned.1.call-update
  57.9 67.4 %reduce-scatter.2.cloned.1.call-done = f32[64,512]{1,0:T(8,128)} async-done(((f32[512,512]{1,0:T(8,128)}), f32[64,512]{1,0:T(8,128)}) %reduce-scatter.2.cloned.1.call-update) | async-done | bytes 131088 | tf_op jit(solution)/shard_map/reduce_scatter | solution.py:25
  (8 shorter events, 0.2 us)
Async XLA Ops:
  6.5 49.6 %copy-start = (bf16[1,800,512]{2,1,0:T(8,128)(2,1)S(1)}, bf16[1,800,512]{2,1,0:T(8,128)(2,1)}, u32[]{:S(2)}) copy-start(bf16[1,800,512]{2,1,0:T(8,128)(2,1)} %param.3) | copy-start | bytes 2457604
  6.5 118.7 %reduce-scatter.2.cloned.1.call-start = ((), (), s32[]{:S(2)}) async-start(), calls=%async_computation.1 | async-start | bytes 1179648 | tf_op jit(solution)/shard_map/reduce_scatter | solution.py:25
  27.0 9.1 %copy-start.3 = (bf16[64,1,800]{0,1,2:T(2,128)(2,1)S(1)}, bf16[64,1,800]{0,1,2:T(2,128)(2,1)}, u32[]{:S(2)}) copy-start(bf16[64,1,800]{0,1,2:T(2,128)(2,1)} %get-tuple-element.8) | copy-start | bytes 307204
  27.0 12.3 %copy-start.2 = (bf16[64,1,800]{0,1,2:T(2,128)(2,1)S(1)}, bf16[64,1,800]{0,1,2:T(2,128)(2,1)}, u32[]{:S(2)}) copy-start(bf16[64,1,800]{0,1,2:T(2,128)(2,1)} %get-tuple-element.7) | copy-start | bytes 307204
  27.0 14.2 %copy-start.1 = (bf16[64,1,800]{0,1,2:T(2,128)(2,1)S(1)}, bf16[64,1,800]{0,1,2:T(2,128)(2,1)}, u32[]{:S(2)}) copy-start(bf16[64,1,800]{0,1,2:T(2,128)(2,1)} %get-tuple-element.12) | copy-start | bytes 307204
  28.9 14.9 %collective-permute-start = (bf16[64,1,800]{2,0,1:T(8,128)(2,1)}, bf16[64,1,800]{2,0,1:T(8,128)(2,1)S(1)}, u32[]{:S(2)}, u32[]{:S(2)}) collective-permute-start(bf16[64,1,800]{2,0,1:T(8,128)(2,1)} %copy.14), channel_id=1, source_target_pairs={{0,4},{4,0},{8,12},{12,8},{16,20},{20,16},{24,28},{28,24},{1,5},{5... | collective-permute-start | bytes 307208 | tf_op jit(solution)/shard_map/ppermute | solution.py:20
  32.2 15.2 %collective-permute-start.1 = (bf16[64,1,800]{2,0,1:T(8,128)(2,1)}, bf16[64,1,800]{2,0,1:T(8,128)(2,1)S(1)}, u32[]{:S(2)}, u32[]{:S(2)}) collective-permute-start(bf16[64,1,800]{2,0,1:T(8,128)(2,1)} %copy.15), channel_id=1, source_target_pairs={{0,8},{4,12},{8,0},{12,4},{16,24},{20,28},{24,16},{28,20},{1,9},{5... | collective-permute-start | bytes 307208 | tf_op jit(solution)/shard_map/ppermute | solution.py:20
  35.6 12.1 %collective-permute-start.2 = (bf16[64,1,800]{2,0,1:T(8,128)(2,1)}, bf16[64,1,800]{2,0,1:T(8,128)(2,1)S(1)}, u32[]{:S(2)}, u32[]{:S(2)}) collective-permute-start(bf16[64,1,800]{2,0,1:T(8,128)(2,1)} %copy.16), channel_id=1, source_target_pairs={{0,12},{4,8},{8,4},{12,0},{16,28},{20,24},{24,20},{28,16},{1,13},{... | collective-permute-start | bytes 307208 | tf_op jit(solution)/shard_map/ppermute | solution.py:20
  36.6 11.1 %collective-permute-start.3 = (bf16[64,1,800]{2,0,1:T(8,128)(2,1)S(1)}, bf16[64,1,800]{2,0,1:T(8,128)(2,1)S(1)}, u32[]{:S(2)}, u32[]{:S(2)}) collective-permute-start(bf16[64,1,800]{2,0,1:T(8,128)(2,1)S(1)} %copy.17), channel_id=1, source_target_pairs={{0,16},{4,20},{8,24},{12,28},{16,0},{20,4},{24,8},{28,12},{1,17},{... | collective-permute-start | bytes 307208 | tf_op jit(solution)/shard_map/ppermute | solution.py:20
  39.9 16.2 %collective-permute-start.4 = (bf16[64,1,800]{2,0,1:T(8,128)(2,1)S(1)}, bf16[64,1,800]{2,0,1:T(8,128)(2,1)S(1)}, u32[]{:S(2)}, u32[]{:S(2)}) collective-permute-start(bf16[64,1,800]{2,0,1:T(8,128)(2,1)S(1)} %copy.18), channel_id=1, source_target_pairs={{0,20},{4,16},{8,28},{12,24},{16,4},{20,0},{24,12},{28,8},{1,21},{... | collective-permute-start | bytes 307208 | tf_op jit(solution)/shard_map/ppermute | solution.py:20
  43.8 12.3 %collective-permute-start.5 = (bf16[64,1,800]{2,0,1:T(8,128)(2,1)}, bf16[64,1,800]{2,0,1:T(8,128)(2,1)S(1)}, u32[]{:S(2)}, u32[]{:S(2)}) collective-permute-start(bf16[64,1,800]{2,0,1:T(8,128)(2,1)} %copy.19), channel_id=1, source_target_pairs={{0,24},{4,28},{8,16},{12,20},{16,8},{20,12},{24,0},{28,4},{1,25},{... | collective-permute-start | bytes 307208 | tf_op jit(solution)/shard_map/ppermute | solution.py:20
  47.5 8.6 %collective-permute-start.6 = (bf16[64,1,800]{2,0,1:T(8,128)(2,1)S(1)}, bf16[64,1,800]{2,0,1:T(8,128)(2,1)S(1)}, u32[]{:S(2)}, u32[]{:S(2)}) collective-permute-start(bf16[64,1,800]{2,0,1:T(8,128)(2,1)S(1)} %copy.20), channel_id=1, source_target_pairs={{0,28},{4,24},{8,20},{12,16},{16,12},{20,8},{24,4},{28,0},{1,29},{... | collective-permute-start | bytes 307208 | tf_op jit(solution)/shard_map/ppermute | solution.py:20
Sparse Core Ops, SparseCore 0:
  58.0 67.2 reduce-scatter.1
